TPU v7x, 256 devices: a whole 4x4x8 slice. The times are simulated.
256 devices in a mesh: section: 8 (over z_lo, core), dp: 32 (over x, y, z_hi).
Axes of the slice: x: 4, y: 4, z: 8 (z_hi: 2, z_lo: 4; z = z_hi * 4 + z_lo), core: 2. Of those that a mesh axis runs over, the one named last changes fastest.
Arguments:
- outputs: bfloat16 [8, 4096, 6144], P('section', 'dp'), may hold values from -6 to 6
- cotangents: bfloat16 [8, 4, 4096, 6144], P('section', None, 'dp'), may hold values from -6 to 6
- gain: float32 [8, 6144], P('section'), may hold values from 0.25 to 1.75
- w_in: bfloat16 [8, 6144, 32], P('section'), may hold values from -0.3125 to 0.3125
- w_out: bfloat16 [8, 32, 32], P('section'), may hold values from -1 to 1
Outputs:
- grad_outputs: bfloat16 [8, 4096, 6144], P('section', 'dp')
- grad_w_in: float32 [8, 6144, 32], P('section')
- grad_w_out: float32 [8, 32, 32], P('section')
- grad_gain: float32 [8, 6144], P('section')
All inputs are finite; a program needn't handle non-finite values.
Results may differ from a plain program's by a relative error of at most 0.03.
Values may be sent and summed in bfloat16 or wider, within the bound.
A program may use at most 128 MiB of HBM per device.

v0:
```python
import jax
import jax.numpy as jnp
from jax import lax
from jax.sharding import PartitionSpec as P


def gelu_back(pre, dhid):
    return jax.vjp(lambda v: jax.nn.gelu(v, approximate=True), pre)[1](dhid)[0]


def layer_dots(dys, rows):
    return lax.dot_general(
        dys, rows, (((2,), (2,)), ((1,), (1,))), preferred_element_type=jnp.float32
    )


def shards(outputs, cotangents, gain, w_in, w_out):
    layers = lax.axis_size("section")
    section_pos = lax.axis_index("section")
    tok = outputs.shape[1]
    dys = cotangents[0]
    x = outputs[0].astype(jnp.float32)
    rinv = lax.rsqrt(jnp.mean(x * x, axis=-1, keepdims=True) + 1e-06)
    normed = x * rinv
    hnorm = (normed * gain[0]).astype(jnp.bfloat16)
    pre = jnp.dot(hnorm, w_in[0], preferred_element_type=jnp.float32)
    hid = jax.nn.gelu(pre, approximate=True).astype(jnp.bfloat16)
    positions = jnp.arange(layers, dtype=jnp.int32)
    keep = (positions <= section_pos).astype(jnp.float32)
    mixw = jnp.dot(hid, w_out[0], preferred_element_type=jnp.float32).reshape(tok, 4, layers) * keep
    found = layer_dots(dys, lax.all_gather(outputs, "section", axis=0, tiled=True))
    dmix = found
    dmix = dmix * keep
    many = tok * lax.axis_size("section") // tok
    total = jnp.zeros((many, tok, dys.shape[2]), jnp.float32)
    for stream in range(4):
        total = total + mixw[:, stream, :].T[:, :, None] * dys[stream].astype(jnp.float32)[None]
    mixed_grad = lax.psum_scatter(
        total.reshape(tok * lax.axis_size("section"), dys.shape[2]).astype(jnp.bfloat16),
        "section",
        scatter_dimension=0,
        tiled=True,
    ).astype(jnp.float32)
    dflat = dmix.reshape(tok, 4 * layers).astype(jnp.bfloat16)
    wout_grad = jnp.einsum("tk,tm->km", hid, dflat, preferred_element_type=jnp.float32)
    dhid = lax.dot_general(
        dflat, w_out[0], (((1,), (1,)), ((), ())), preferred_element_type=jnp.float32
    )
    dpre = gelu_back(pre, dhid).astype(jnp.bfloat16)
    win_grad = jnp.einsum("td,tk->dk", hnorm, dpre, preferred_element_type=jnp.float32)
    dh = lax.dot_general(
        dpre, w_in[0], (((1,), (1,)), ((), ())), preferred_element_type=jnp.float32
    )
    gain_grad = jnp.sum(dh * normed, axis=0)
    dn = dh * gain[0]
    gate_grad = rinv * (dn - normed * jnp.mean(dn * normed, axis=-1, keepdims=True))
    win_sum, wout_sum, gain_sum = (
        lax.psum(win_grad.astype(jnp.bfloat16), "dp").astype(jnp.float32),
        lax.psum(wout_grad.astype(jnp.bfloat16), "dp").astype(jnp.float32),
        lax.psum(gain_grad.astype(jnp.bfloat16), "dp").astype(jnp.float32),
    )
    grad_outputs = (mixed_grad + gate_grad).astype(jnp.bfloat16)[None]
    return (grad_outputs, win_sum[None], wout_sum[None], gain_sum[None])


def solution(mesh):
    placed = (
        P("section", "dp", None),
        P("section", None, "dp", None),
        P("section", None),
        P("section", None, None),
        P("section", None, None),
    )
    return jax.shard_map(
        shards,
        mesh=mesh,
        in_specs=placed,
        out_specs=(
            P("section", "dp", None),
            P("section", None, None),
            P("section", None, None),
            P("section", None),
        ),
        check_vma=False,
    )
```

profile of v0, /device:TPU:1, one launch (start us, length us, event | category | flops | bytes accessed | tf_op | source)
XLA Modules:
  0.0 723.3 jit_solution(11535965767690969658)
XLA Ops:
  7.2 0.0 copy-start
  7.2 0.0 copy-start.1
  7.2 0.0 copy-start.2
  7.2 0.0 all-gather.2.cloned.1.call-start
  7.2 0.7 all-gather.2.cloned.1.call-update
  7.9 0.0 all-reduce.3.cloned.1.call-start
  8.0 0.8 copy.17
  8.8 1.8 fusion.21
  10.6 0.0 copy-done
  10.6 0.0 copy-done.1
  10.6 0.0 copy-done.2
  10.6 0.7 fusion.25
  11.3 7.9 %bitcast_convert_fusion.3 = (f32[128,6144]{1,0:T(8,128)}, f32[128,6144]{1,0:T(8,128)}, f32[128,6144]{1,0:T(8,128)}, f32[128,6144]{1,0:T(8,128)}) fusion(bf16[1,4,128,6144]{3,2,1,0:T(8,128)(2,1)} %param.6), kind=kLoop, calls=%fused_computation.37 | loop fusion | flops 3145728 | bytes 18874368 | tf_op jit(solution)/shard_map/convert_element_type | solution.py:37
  19.2 125.4 %all-gather.2.cloned.1.call-done = bf16[8,128,6144]{2,1,0:T(8,128)(2,1)} async-done(((bf16[1,128,6144]{2,1,0:T(8,128)(2,1)}), bf16[8,128,6144]{2,1,0:T(8,128)(2,1)}) %all-gather.2.cloned.1.call-update) | async-done | bytes 12582928 | tf_op jit(solution)/shard_map/all_gather | solution.py:31
  144.6 0.0 copy-start.3
  144.6 20.2 %fusion.4 = f32[128,4,8]{2,1,0:T(4,128)S(1)} fusion(bf16[8,128,6144]{2,1,0:T(8,128)(2,1)} %all-gather.2.cloned.1.call-done, bf16[4,128,6144]{2,1,0:T(8,128)(2,1)} %bitcast.130), kind=kOutput, calls=%fused_computation.8 | convolution fusion | flops 50331648 | bytes 18890752 | tf_op jit(solution)/shard_map/dot_general | solution.py:12
  164.8 0.1 copy.20
  164.9 0.0 copy-done.3
  164.9 0.2 fusion.43
  165.1 1.4 fusion.6
  166.5 0.0 all-reduce.3.cloned.1.call-update
  166.6 0.2 reduce-scatter.2.cloned.1.call-start
  166.8 0.1 convolution_multiply_fusion
  166.9 17.1 %fusion.1 = bf16[1024,6144]{1,0:T(8,128)(2,1)} fusion(f32[128,6144]{1,0:T(8,128)} %get-tuple-element.11, f32[1024]{0:T(1024)S(1)} %get-tuple-element.13, f32[128,6144]{1,0:T(8,128)} %get-tuple-element.9, f32[1024]{0:T(1024)S(1)} %get-tuple-element.14, f32[128,6144]{1,0:T(8,128)} %get-tuple-element.10, f32[1024]{0:T(1024)S(1)} %get-tuple-element.15, ...), kind=kLoop, calls=%fused_computation.2 | loop fusion | flops 50331648 | bytes 25182208 | tf_op jit(solution)/shard_map/convert_element_type | solution.py:39
  184.0 0.0 reduce-scatter.2.cloned.1.call-update
  184.0 2.7 fusion.20
  186.7 0.2 fusion.33
  186.9 200.1 %all-reduce = (bf16[1,32,32]{2,1,0:T(8,128)(2,1)S(1)}, bf16[1,6144]{1,0:T(2,128)(2,1)S(1)}) all-reduce(bf16[1,32,32]{2,1,0:T(8,128)(2,1)S(1)} %fusion.33, bf16[1,6144]{1,0:T(2,128)(2,1)S(1)} %broadcast_in_dim.38), channel_id=1, replica_groups=mesh['section'=8,'dp'=32] {'dp'}, use_global_device_ids=true, to_apply=%region_4.0 | all-reduce | flops 7168 | bytes 28672 | tf_op jit(solution)/shard_map/psum | solution.py:59
  387.0 0.6 broadcast_in_dim.39
  387.7 0.6 broadcast_in_dim.37
  388.3 173.7 %all-reduce.3.cloned.1.call-done = bf16[1,6144,32]{1,2,0:T(8,128)(2,1)} async-done(((bf16[1,6144,32]{1,2,0:T(8,128)(2,1)}), bf16[1,6144,32]{1,2,0:T(8,128)(2,1)}) %all-reduce.3.cloned.1.call-update) | async-done | bytes 393232 | tf_op jit(solution)/shard_map/psum | solution.py:58
  562.0 1.9 broadcast_in_dim.35
  563.9 148.4 %reduce-scatter.2.cloned.1.call-done = bf16[128,6144]{1,0:T(8,128)(2,1)} async-done(((bf16[1024,6144]{1,0:T(8,128)(2,1)}), bf16[128,6144]{1,0:T(8,128)(2,1)}) %reduce-scatter.2.cloned.1.call-update) | async-done | bytes 1572880 | tf_op jit(solution)/shard_map/reduce_scatter | solution.py:38
  712.3 4.5 fusion.28
  (5 shorter events, 0.0 us)
Async XLA Ops:
  7.2 3.4 copy-start
  7.2 3.4 copy-start.1
  7.2 3.4 copy-start.2
  7.2 137.4 %all-gather.2.cloned.1.call-start = ((), (), s32[]{:S(2)}) async-start(), calls=%async_computation.2 | async-start | bytes 14155776 | tf_op jit(solution)/shard_map/all_gather | solution.py:31
  7.9 554.1 %all-reduce.3.cloned.1.call-start = ((), (), s32[]{:S(2)}) async-start(), calls=%async_computation.3 | async-start | bytes 786432 | tf_op jit(solution)/shard_map/psum | solution.py:58
  144.6 20.2 %copy-start.3 = (bf16[1,32,32]{2,1,0:T(8,128)(2,1)S(1)}, bf16[1,32,32]{2,1,0:T(8,128)(2,1)}, u32[]{:S(2)}) copy-start(bf16[1,32,32]{2,1,0:T(8,128)(2,1)} %param.9) | copy-start | bytes 6148
  166.6 545.8 %reduce-scatter.2.cloned.1.call-start = ((), (), s32[]{:S(2)}) async-start(), calls=%async_computation.1 | async-start | bytes 14155776 | tf_op jit(solution)/shard_map/reduce_scatter | solution.py:38
Sparse Core Ops, SparseCore 0:
  9.8 134.7 all-gather.1
  166.7 395.2 all-reduce.2
  564.7 147.5 reduce-scatter.1
where the time goes:
time: 725 us; the launch traced here: 723 us
  waiting for transfers between devices  448 us (62%)
  blocking collectives  200 us (28%)
  other arithmetic  34.4 us (5%)
  matrix products  25.5 us (4%)
  between operations  13.8 us (2%)
    psum x1, blocking collectives, shards(): lax.psum(wout_grad.astype(jnp.bfloat16), 'dp').astype(jnp.float32)  200 us
    psum x1, waiting for transfers between devices, shards(): lax.psum(win_grad.astype(jnp.bfloat16), 'dp').astype(jnp.float32)  174 us
    reduce_scatter x1, waiting for transfers between devices, shards(): lax.psum_scatter(total.reshape(tok * lax.axis_size('section'), dys.shape[...  148 us
    all_gather x1, waiting for transfers between devices, shards(): lax.all_gather(outputs, 'section', axis=0, tiled=True)  125 us
    dot_general x1, matrix products, layer_dots(): lax.dot_general(dys, rows, (((2,), (2,)), ((1,), (1,))), preferred_elemen...  20.2 us
    convert_element_type x1, other arithmetic, shards(): total.reshape(tok * lax.axis_size('section'), dys.shape[2])  17.1 us
  transfers between devices with their start and end apart: 3, of which 3 were waited for; matrix products, arithmetic and copies ran while one was open for 5% of the time, Pallas kernels for 0%

commit v1 on v0

v1 whole, which is shorter than its diff:
```python
import functools

import jax
import jax.numpy as jnp
from jax import lax
from jax.experimental import pallas as pl
from jax.experimental.pallas import tpu as pltpu
from jax.sharding import PartitionSpec as P

ND = 12
NB = 1
LAG = 3
PF = 3
PF_TOP = 6
MESH = pl.DeviceIdType.MESH
F32 = jnp.float32
BF16 = jnp.bfloat16
C0 = 0.7978845608028654
C1 = 0.044715


def gelu(v):
    return 0.5 * v * (1.0 + jnp.tanh(C0 * (v + C1 * v * v * v)))


def gelu_slope(v):
    t = jnp.tanh(C0 * (v + C1 * v * v * v))
    return 0.5 * (1.0 + t) + 0.5 * v * (1.0 - t * t) * (C0 * (1.0 + 3.0 * C1 * v * v))


def nt(a, b):
    return lax.dot_general(a, b, (((1,), (1,)), ((), ())), preferred_element_type=F32)


def tn(a, b):
    return lax.dot_general(a, b, (((0,), (0,)), ((), ())), preferred_element_type=F32)


def iota(shape, dim):
    return lax.broadcasted_iota(jnp.int32, shape, dim)


def kernel(
    nq, x_ref, cot_ref, gain_ref, win_ref, wout_ref,
    out_ref, gwin_ref, gwout_ref, ggain_ref,
    X, HN, OUT, GG, G, C, CB, PB, R, SR, PS, A, A3, ACC, ACC3,
    PRE, RI, MS, WF, WS, W3, DMT, DM, DMB, D3X, DP, WO,
    PK, RB, ZF, ZS, ZR, AG,
    x_sem, out_sem, lg_sem, lc_sem, sg_s, sg_r, sc_s, sc_r, up_s, up_r, fw_s, fw_r,
    dn_s, dn_r, cb_s, cb_r, ss_s, ss_r, w_s, w_r, w3_s, w3_r, dm_s, dm_r, d3_s, d3_r,
    rs_s, rs_r, z_s, z_r, ag_s, ag_r,
):
    D = x_ref.shape[1]
    DC = D // ND
    CW = D // nq
    s = lax.axis_index("section")
    dp = lax.axis_index("dp")
    k = s // 2
    c = s % 2
    q = dp // 2
    zh = dp % 2
    sib = s + 1 - 2 * c
    top = k == 3
    below_top = k < 3

    def half(h):
        return pl.ds(pl.multiple_of(h * 64, 64), 64)

    def cols(d):
        return pl.ds(pl.multiple_of(d * DC, 128), DC)

    def wide(p):
        return pl.ds(pl.multiple_of(p * CW, 128), CW)

    def send(src, dst, ss, rs, to):
        return pltpu.make_async_remote_copy(
            src_ref=src, dst_ref=dst, send_sem=ss, recv_sem=rs, device_id=to, device_id_type=MESH
        )

    def sec(n):
        return {"section": n}

    def load_x():
        return pltpu.make_async_copy(x_ref, X, x_sem)

    def load_g(d):
        return pltpu.make_async_copy(x_ref.at[half(c), cols(d)], G.at[d, s], lg_sem.at[d])

    def load_c(d):
        return pltpu.make_async_copy(
            cot_ref.at[:, half(c), cols(d)], C.at[d, pl.ds(4 * c, 4)], lc_sem.at[d]
        )

    def sib_g(d):
        return send(x_ref.at[half(1 - c), cols(d)], G.at[d, s], sg_s.at[d], sg_r.at[d], sec(sib))

    def sib_c(d):
        return send(
            cot_ref.at[:, half(1 - c), cols(d)], C.at[d, pl.ds(4 * c, 4)], sc_s.at[d], sc_r.at[d], sec(sib)
        )

    def up_own(d, h, source):
        to = jnp.minimum(2 * k + 2 + h, 7)
        return send(x_ref.at[half(h), cols(d)], G.at[d, s], up_s.at[d, h], up_r.at[d, source], sec(to))

    def up_fwd(d, m):
        pair = pl.ds(2 * m, 2)
        return send(
            G.at[d, pair], G.at[d, pair], fw_s.at[d, m], fw_r.at[d, m], sec(jnp.minimum(s + 2, 7))
        )

    def down(d, m):
        pair = pl.ds(2 * m, 2)
        return send(
            PB.at[d, pair], R.at[d, pair], dn_s.at[d, m], dn_r.at[d, m], sec(jnp.maximum(s - 2, 0))
        )

    def hand(d, h, source):
        return send(
            cot_ref.at[:, half(h), cols(d)], CB.at[d, pl.ds(4 * c, 4)], cb_s.at[d, h], cb_r.at[d, source],
            sec(4 + h),
        )

    def sib_s(d):
        return send(PB.at[d, sib], SR.at[d], ss_s.at[d], ss_r.at[d], sec(sib))

    def sib_w():
        return send(WF.at[half(1 - c)], WS.at[c], w_s, w_r, sec(sib))

    def top_w(h, source):
        return send(WF.at[half(h)], W3.at[c], w3_s.at[h], w3_r.at[source], sec(4 + h))

    def sib_dm():
        return send(DMT.at[1 - c], DM.at[c], dm_s, dm_r, sec(sib))

    def top_dm(cc, source):
        return send(D3X.at[cc], DMB.at[c], d3_s.at[cc], d3_r.at[source], sec(6 + cc))

    def peer(p):
        return {"dp": 2 * p + zh}

    def rs(p, source):
        return send(PK.at[p], RB.at[q], rs_s.at[p], rs_r.at[source], peer(p))

    def swap():
        return send(ZS, ZR, z_s, z_r, {"dp": dp + 1 - 2 * zh})

    def ag(p, source):
        return send(AG.at[q], AG.at[q], ag_s.at[p], ag_r.at[source], peer(p))

    def around(o):
        return lax.rem(q + o, nq)

    load_x().start()

    def first_loads(d, carry):
        load_c(d).start()
        load_g(d).start()
        return carry

    lax.fori_loop(0, PF, first_loads, 0)

    barrier = pltpu.get_barrier_semaphore()

    def greet(to):
        pl.semaphore_signal(barrier, inc=1, device_id=to, device_id_type=MESH)

    greet(sec(sib))
    for h in range(2):

        @pl.when(below_top)
        def _():
            greet(sec(jnp.minimum(2 * k + 2 + h, 7)))

        @pl.when(k > 0)
        def _():
            greet(sec(jnp.maximum(2 * k - 2 + h, 0)))

    def greet_peer(o, carry):
        greet(peer(around(o)))
        return carry

    lax.fori_loop(1, nq, greet_peer, 0)
    greet({"dp": dp + 1 - 2 * zh})
    sides = jnp.where(below_top, 2, 0) + jnp.where(k > 0, 2, 0)
    pl.semaphore_wait(barrier, nq + 1 + sides)

    def goes_up(d):
        return jnp.logical_and(below_top, jnp.logical_or(k < 2, d >= NB))

    def start_up(d):
        @pl.when(goes_up(d))
        def _():
            for h in range(2):
                up_own(d, h, c).start()

    @pl.when(top)
    def _():
        for d in range(NB):
            for h in range(2):
                hand(d, h, c).start()

    def first_sends(d, carry):
        start_up(d)
        sib_c(d).start()
        sib_g(d).start()
        return carry

    lax.fori_loop(0, PF, first_sends, 0)
    ahead = jnp.where(k == 2, PF_TOP, PF)

    def more_up(d, carry):
        start_up(d)
        return carry

    lax.fori_loop(PF, ahead, more_up, 0)

    @pl.when(top)
    def _():
        for d in range(NB):
            for j in range(6):
                G[d, j] = jnp.zeros((64, DC), BF16)

    load_x().wait()
    step = D // 6

    def norm_rows(r, carry):
        rows = pl.ds(pl.multiple_of(r * 16, 16), 16)
        total = jnp.zeros((16, 1), F32)
        for p in range(6):
            v = X[rows, p * step : (p + 1) * step].astype(F32)
            total = total + jnp.sum(v * v, axis=1, keepdims=True)
        rinv = lax.rsqrt(total * (1.0 / D) + 1e-06)
        RI[rows, :] = rinv
        for p in range(6):
            at = slice(p * step, (p + 1) * step)
            HN[rows, at] = (X[rows, at].astype(F32) * rinv * gain_ref[:, at]).astype(BF16)
        return carry

    lax.fori_loop(0, 8, norm_rows, 0)
    pre = nt(HN[...], win_ref[...])
    PRE[...] = pre
    hid = gelu(pre).astype(BF16)
    mixw = jnp.dot(hid, wout_ref[...], preferred_element_type=F32)
    mixw = jnp.where((iota((128, 32), 1) & 7) <= s, mixw, 0.0)
    WF[...] = jnp.zeros((128, 128), BF16)
    WF[:, 0:32] = mixw.astype(BF16)
    sib_w().start()

    @pl.when(top)
    def _():
        for h in range(2):
            top_w(h, c).start()

    WS[c] = WF[half(c), :]
    for g in range(2):
        ACC[g] = jnp.zeros((256, 256), F32)
    sib_w().wait_recv()

    def spread(W, A):
        row = iota((256, 128), 0)
        lane = iota((256, 128), 1)
        pick = jnp.logical_and(lane < 32, (lane & 7) == (row >> 5))
        srow = iota((128, 256), 0)
        scol = iota((128, 256), 1)
        same = (iota((256, 256), 0) & 31) == (iota((256, 256), 1) & 31)
        for g in range(2):
            total = jnp.zeros((256, 256), F32)
            for cc in range(2):
                w = W[cc, 32 * g : 32 * g + 32, :].astype(F32)
                w = jnp.where(pick, jnp.concatenate([w] * 8, axis=0), 0.0).astype(BF16)
                place = jnp.logical_and(srow < 32, (scol >> 5) == 4 * cc + (srow >> 3))
                total = total + jnp.dot(w, jnp.where(place, 1.0, 0.0).astype(BF16), preferred_element_type=F32)
            A[g] = jnp.where(same, total, 0.0).astype(BF16)

    spread(WS, A)

    def group(ref, d, g):
        return ref[d, :, 32 * g : 32 * g + 32, :].reshape(256, DC)

    def stage_part(d):
        handed = d < NB
        for g in range(2):
            PS[g] = jnp.dot(A[g], group(C, d, g), preferred_element_type=F32)

        @pl.when(jnp.logical_and(k == 2, handed))
        def _():
            for a in range(2):
                hand(d, 0, a).wait_recv()
            for g in range(2):
                PS[g] = PS[g] + jnp.dot(A3[g], group(CB, d, g), preferred_element_type=F32)
                ACC3[g] = ACC3[g] + nt(group(CB, d, g), group(G, d, g))

        takes = jnp.logical_and(below_top, jnp.logical_or(k < 2, d >= NB))
        for m in range(4):

            def keep(with_r):
                for g in range(2):
                    rows = slice(32 * g, 32 * g + 32)
                    own = PS[g, 64 * m : 64 * m + 64, :].reshape(2, 32, DC)
                    if with_r:
                        own = own + R[d, 2 * m : 2 * m + 2, rows, :].astype(F32)
                    PB[d, 2 * m : 2 * m + 2, rows, :] = own.astype(BF16)

            if m < 3:

                @pl.when(jnp.logical_and(m <= k, takes))
                def _():
                    down(d, m).wait_recv()
                    keep(True)

            @pl.when(jnp.logical_and(m <= k, jnp.logical_not(takes)))
            def _():
                keep(False)

            if m < 3:

                @pl.when(jnp.logical_and(m < k, jnp.logical_or(below_top, d >= NB)))
                def _():
                    down(d, m).start()

            @pl.when(m == k)
            def _():
                sib_s(d).start()

    def stage_gather(d):
        for m in (2, 1, 0):

            @pl.when(jnp.logical_and(m < k, jnp.logical_or(below_top, d >= NB)))
            def _():
                @pl.when(m == k - 1)
                def _():
                    for a in range(2):
                        up_own(d, 0, a).wait_recv()

                if m < 2:

                    @pl.when(m < k - 1)
                    def _():
                        up_fwd(d, m).wait_recv()

                    @pl.when(goes_up(d))
                    def _():
                        up_fwd(d, m).start()

    def stage_dmix(d):
        load_g(d).wait()
        sib_g(d).wait_recv()
        for g in range(2):
            ACC[g] = ACC[g] + nt(group(C, d, g), group(G, d, g))

    def extract(acc, low, rise, into):
        row = iota((256, 256), 0)
        col = iota((256, 256), 1)
        ok = jnp.logical_and((row & 31) == (col & 31), (col >> 5) <= low + rise * (row >> 7))
        srow = iota((256, 128), 0)
        lane = iota((256, 128), 1)
        place = jnp.where(jnp.logical_and(lane < 32, (lane & 7) == (srow >> 5)), 1.0, 0.0)
        mine = (lane >> 3) == ((srow >> 5) & 3)
        for g in range(2):
            v = jnp.where(ok, acc[g], 0.0)
            v = jnp.dot(v, place, precision=lax.Precision.HIGHEST, preferred_element_type=F32)
            v = jnp.where(mine, v, 0.0)
            for cc in range(2):
                into[cc, 32 * g : 32 * g + 32, :] = sum(
                    v[128 * cc + 32 * st : 128 * cc + 32 * st + 32] for st in range(4)
                )

    def stage_grads():
        extract(ACC, 2 * k, 1, DMT)
        sib_dm().start()
        DM[c] = DMT[c]
        sib_dm().wait_recv()

        @pl.when(top)
        def _():
            for a in range(2):
                top_dm(0, a).wait_recv()
            DM[...] = DM[...] + DMB[...]

        dflat = DM[...].reshape(128, 128)[:, 0:32].astype(BF16)
        pre = PRE[...]
        dpre = (gelu_slope(pre) * nt(dflat, wout_ref[...])).astype(BF16)
        DP[...] = dpre
        WO[...] = jnp.zeros((32, CW), F32)
        WO[:, 0:32] = tn(gelu(pre).astype(BF16), dflat)
        MS[...] = jnp.zeros((128, 1), F32)

        def pack(o, carry):
            p = around(o)
            at = wide(p)
            dh = jnp.dot(DP[...], win_ref[:, at], preferred_element_type=F32)
            t = dh * (X[:, at].astype(F32) * RI[...])
            MS[...] = MS[...] + jnp.sum(t * gain_ref[:, at], axis=1, keepdims=True)
            PK[p, 0:32, :] = tn(DP[...], HN[:, at]).astype(BF16)
            rid = iota((16, CW), 0)
            per = 32 // nq
            tile = jnp.where(rid == 0, jnp.sum(t, axis=0, keepdims=True), 0.0)
            for e in range(per):
                tile = jnp.where(rid == 1 + e, WO[pl.ds(per * p + e, 1), :], tile)
            PK[p, 32:48, :] = tile.astype(BF16)

            @pl.when(o < nq)
            def _():
                rs(p, q).start()

            return carry

        lax.fori_loop(1, nq + 1, pack, 0)

        def gate(p, carry):
            at = wide(p)
            dn = jnp.dot(DP[...], win_ref[:, at], preferred_element_type=F32) * gain_ref[:, at]
            normed = X[:, at].astype(F32) * RI[...]
            GG[:, at] = RI[...] * (dn - normed * (MS[...] * (1.0 / D)))
            return carry

        lax.fori_loop(0, nq, gate, 0)

    def stage_sum():
        ZF[...] = PK[q].astype(F32)

        def add(o, carry):
            p = around(o)
            rs(0, p).wait_recv()
            ZF[...] = ZF[...] + RB[p].astype(F32)
            return carry

        lax.fori_loop(1, nq, add, 0)
        ZS[...] = ZF[...].astype(BF16)
        swap().start()

    def stage_share():
        swap().wait_recv()
        AG[q] = (ZS[...].astype(F32) + ZR[...].astype(F32)).astype(BF16)

        def give(o, carry):
            ag(around(o), q).start()
            return carry

        lax.fori_loop(1, nq, give, 0)

    @pl.when(k == 2)
    def _():
        for a in range(2):
            top_w(0, a).wait_recv()
        spread(W3, A3)
        for g in range(2):
            ACC3[g] = jnp.zeros((256, 256), F32)

    lead_part = jnp.where(top, 0, LAG)
    lead_dmix = jnp.where(top, LAG, 0)
    tail = ND + lead_dmix

    def body(i, carry):
        @pl.when(i + PF < ND)
        def _():
            d = i + PF
            load_c(d).start()
            load_g(d).start()
            sib_c(d).start()
            sib_g(d).start()

        @pl.when(i + ahead < ND)
        def _():
            start_up(i + ahead)

        @pl.when(i < ND)
        def _():
            load_c(i).wait()
            sib_c(i).wait_recv()

        @pl.when(jnp.logical_and(k == 2, i == NB + LAG))
        def _():
            extract(ACC3, 5, 0, D3X)
            for cc in range(2):
                top_dm(cc, c).start()

        pl.when(i == tail)(stage_grads)
        pl.when(i == tail + 1)(stage_sum)
        pl.when(i == tail + 2)(stage_share)
        d = i - lead_part

        @pl.when(jnp.logical_and(d >= 0, d < ND))
        def _():
            stage_part(d)

        e = i - lead_dmix

        @pl.when(jnp.logical_and(e >= 0, e < ND))
        def _():
            stage_gather(e)
            stage_dmix(e)

        return carry

    lax.fori_loop(0, ND + LAG + 3, body, 0)

    def finish(d, carry):
        sib_s(d).wait_recv()
        at = cols(d)
        OUT[half(c), at] = (PB[d, s].astype(F32) + GG[half(c), at]).astype(BF16)
        OUT[half(1 - c), at] = (SR[d].astype(F32) + GG[half(1 - c), at]).astype(BF16)
        return carry

    lax.fori_loop(0, ND, finish, 0)
    store = pltpu.make_async_copy(OUT, out_ref, out_sem)
    store.start()

    def unpack(o, carry):
        p = around(o)

        @pl.when(o < nq)
        def _():
            ag(0, p).wait_recv()

        at = wide(p)
        gwin_ref[:, at] = AG[p, 0:32, :].astype(F32)
        extra = AG[p, 32:48, :].astype(F32)
        ggain_ref[:, at] = extra[0:1]
        per = 32 // nq
        for e in range(per):
            gwout_ref[pl.ds(per * p + e, 1), :] = extra[1 + e : 2 + e, 0:32]
        return carry

    lax.fori_loop(1, nq + 1, unpack, 0)

    def drain(d, carry):
        sib_c(d).wait_send()
        sib_g(d).wait_send()
        sib_s(d).wait_send()

        @pl.when(goes_up(d))
        def _():
            for h in range(2):
                up_own(d, h, c).wait_send()
            for m in range(2):

                @pl.when(m < k)
                def _():
                    up_fwd(d, m).wait_send()

        for m in range(3):

            @pl.when(jnp.logical_and(m < k, jnp.logical_or(below_top, d >= NB)))
            def _():
                down(d, m).wait_send()

        return carry

    lax.fori_loop(0, ND, drain, 0)
    sib_w().wait_send()
    sib_dm().wait_send()

    @pl.when(top)
    def _():
        for h in range(2):
            top_w(h, c).wait_send()
            for d in range(NB):
                hand(d, h, c).wait_send()

    @pl.when(k == 2)
    def _():
        for cc in range(2):
            top_dm(cc, c).wait_send()

    def drain_peer(o, carry):
        p = around(o)
        rs(p, q).wait_send()
        ag(p, q).wait_send()
        return carry

    lax.fori_loop(1, nq, drain_peer, 0)
    swap().wait_send()
    store.wait()


def shards(outputs, cotangents, gain, w_in, w_out):
    D = outputs.shape[2]
    nq = lax.axis_size("dp") // 2
    DC = D // ND
    CW = D // nq
    dma = pltpu.SemaphoreType.DMA
    any_space = pl.BlockSpec(memory_space=pl.ANY)
    vmem = pl.BlockSpec(memory_space=pltpu.VMEM)
    scratch = [
        pltpu.VMEM((128, D), BF16),
        pltpu.VMEM((128, D), BF16),
        pltpu.VMEM((128, D), BF16),
        pltpu.VMEM((128, D), F32),
        pltpu.VMEM((ND, 8, 64, DC), BF16),
        pltpu.VMEM((ND, 8, 64, DC), BF16),
        pltpu.VMEM((NB, 8, 64, DC), BF16),
        pltpu.VMEM((ND, 8, 64, DC), BF16),
        pltpu.VMEM((ND, 6, 64, DC), BF16),
        pltpu.VMEM((ND, 64, DC), BF16),
        pltpu.VMEM((2, 256, DC), F32),
        pltpu.VMEM((2, 256, 256), BF16),
        pltpu.VMEM((2, 256, 256), BF16),
        pltpu.VMEM((2, 256, 256), F32),
        pltpu.VMEM((2, 256, 256), F32),
        pltpu.VMEM((128, 32), F32),
        pltpu.VMEM((128, 1), F32),
        pltpu.VMEM((128, 1), F32),
        pltpu.VMEM((128, 128), BF16),
        pltpu.VMEM((2, 64, 128), BF16),
        pltpu.VMEM((2, 64, 128), BF16),
        pltpu.VMEM((2, 64, 128), F32),
        pltpu.VMEM((2, 64, 128), F32),
        pltpu.VMEM((2, 64, 128), F32),
        pltpu.VMEM((2, 64, 128), F32),
        pltpu.VMEM((128, 32), BF16),
        pltpu.VMEM((32, CW), F32),
        pltpu.VMEM((nq, 48, CW), BF16),
        pltpu.VMEM((nq, 48, CW), BF16),
        pltpu.VMEM((48, CW), F32),
        pltpu.VMEM((48, CW), BF16),
        pltpu.VMEM((48, CW), BF16),
        pltpu.VMEM((nq, 48, CW), BF16),
        dma, dma, dma((ND,)), dma((ND,)),
        dma((ND,)), dma((ND,)), dma((ND,)), dma((ND,)),
        dma((ND, 2)), dma((ND, 2)), dma((ND, 2)), dma((ND, 2)),
        dma((ND, 3)), dma((ND, 3)), dma((NB, 2)), dma((NB, 2)),
        dma((ND,)), dma((ND,)), dma, dma, dma((2,)), dma((2,)),
        dma, dma, dma((2,)), dma((2,)),
        dma((nq,)), dma((nq,)), dma, dma, dma((nq,)), dma((nq,)),
    ]
    grad, gwin, gwout, ggain = pl.pallas_call(
        functools.partial(kernel, nq),
        out_shape=(
            jax.ShapeDtypeStruct((128, D), BF16),
            jax.ShapeDtypeStruct((32, D), F32),
            jax.ShapeDtypeStruct((32, 32), F32),
            jax.ShapeDtypeStruct((1, D), F32),
        ),
        in_specs=[any_space, any_space, vmem, vmem, vmem],
        out_specs=(any_space, vmem, vmem, vmem),
        scratch_shapes=scratch,
        name="dense_back",
        compiler_params=pltpu.CompilerParams(
            collective_id=0, has_side_effects=True, vmem_limit_bytes=56 << 20
        ),
    )(outputs[0], cotangents[0], gain, w_in[0].T, w_out[0])
    return grad[None], gwin.T[None], gwout[None], ggain


def solution(mesh):
    placed = (
        P("section", "dp", None),
        P("section", None, "dp", None),
        P("section", None),
        P("section", None, None),
        P("section", None, None),
    )
    return jax.shard_map(
        shards,
        mesh=mesh,
        in_specs=placed,
        out_specs=(
            P("section", "dp", None),
            P("section", None, None),
            P("section", None, None),
            P("section", None),
        ),
        check_vma=False,
    )
```

time: 725 us -> 183 us (0.25)
  waiting for transfers between devices: 448 us -> 0 us
  blocking collectives: 200 us -> 0 us
  Pallas kernels: 0 us -> 178 us
  other arithmetic: 34.4 us -> 0 us
  matrix products: 25.5 us -> 0 us
  between operations: 13.8 us -> 0.65 us
    psum x1 -> x0, blocking collectives: 200 us -> none  [shards(): lax.psum(wout_grad.astype(jnp.bfloat16), 'dp').astype(jnp.float32)]
    pallas_call x0 -> x1, Pallas kernels: none -> 178 us  [shards(): pl.pallas_call(functools.partial(kernel, nq), out_shape=(jax.ShapeDtypeSt...]
    psum x1 -> x0, waiting for transfers between devices: 174 us -> none  [shards(): lax.psum(win_grad.astype(jnp.bfloat16), 'dp').astype(jnp.float32)]
    reduce_scatter x1 -> x0, waiting for transfers between devices: 148 us -> none  [shards(): lax.psum_scatter(total.reshape(tok * lax.axis_size('section'), dys.shape[...]
    all_gather x1 -> x0, waiting for transfers between devices: 125 us -> none  [shards(): lax.all_gather(outputs, 'section', axis=0, tiled=True)]
    dot_general x7 -> x0, matrix products: 25.5 us -> none  [the longest x1 20.2 us: layer_dots(): lax.dot_general(dys, rows, (((2,), (2,)), ((1,), (1,))), preferred_elemen...]
    convert_element_type x3 -> x0, other arithmetic: 25 us -> none  [the longest x1 17.1 us: shards(): total.reshape(tok * lax.axis_size('section'), dys.shape[2])]
    broadcast_in_dim x4 -> x0, other arithmetic: 7.65 us -> none  [the longest x1 4.48 us: shards(): grad_outputs = (mixed_grad + gate_grad).astype(jnp.bfloat16)[None]]
  transfers between devices with their start and end apart: 3 -> 0, of which waited for: 3 -> 0; matrix products, arithmetic and copies ran while one was open for 5% -> 0% of each run, Pallas kernels for 0% -> 0%
where the time goes in v1:
time: 183 us
  Pallas kernels  178 us (97%)
  local copies, waits for them, and re-layouts  4.87 us (3%)
    pallas_call x1, Pallas kernels, shards(): pl.pallas_call(functools.partial(kernel, nq), out_shape=(jax.ShapeDtypeSt...  178 us
    unnamed x10, local copies, waits for them, and re-layouts  4.87 us

profile of v1, /device:TPU:1, one launch (start us, length us, event | category | flops | bytes accessed | tf_op | source)
XLA Modules:
  0.0 183.1 jit_solution(16532906182352864914)
XLA Ops:
  0.6 177.6 %dense_back.1 = (bf16[128,6144]{1,0:T(8,128)(2,1)}, f32[32,6144]{1,0:T(8,128)}, f32[32,32]{1,0:T(8,128)}, f32[1,6144]{1,0:T(1,128)}) custom-call(bf16[128,6144]{1,0:T(8,128)(2,1)} %bitcast.13, bf16[4,128,6144]{2,1,0:T(8,128)(2,1)} %bitcast.11, f32[1,6144]{1,0:T(1,128)} %gain_ref.1, bf16[32,6144]{1,0:T(8,128)(2,1)} %bitcast.15, bf16[32,32]{1,0:T(8,128)(2,1)} %bitcast.17), custom_call_target="tpu_custom_call" | custom-call | tf_op jit(solution)/shard_map/dense_back/pallas_call | solution.py:628
  178.2 0.0 copy-start
  178.3 2.8 %copy.13 = bf16[1,128,6144]{2,1,0:T(8,128)(2,1)} copy(bf16[1,128,6144]{2,1,0:T(8,128)(2,1)} %bitcast.12) | data formatting | bytes 3145728
  181.0 0.0 copy-done
  181.0 0.0 copy-start.2
  181.0 0.0 copy-start.1
  181.0 0.9 copy.14
  181.9 0.0 copy-done.2
  181.9 0.6 copy.15
  182.5 0.0 copy-done.1
  182.5 0.6 copy.16
Async XLA Ops:
  178.2 2.8 %copy-start = (f32[32,6144]{1,0:T(8,128)S(1)}, f32[32,6144]{1,0:T(8,128)}, u32[]{:S(2)}) copy-start(f32[32,6144]{1,0:T(8,128)} %get-tuple-element.9) | copy-start | bytes 2359300
  181.0 0.9 copy-start.2
  181.0 1.5 copy-start.1

commit v2 on v1

--- a/solution.py
+++ b/solution.py
@@ -9,7 +9,6 @@
 
 ND = 12
 NB = 1
-LAG = 3
 PF = 3
 PF_TOP = 6
 MESH = pl.DeviceIdType.MESH
@@ -215,6 +214,11 @@
 
     lax.fori_loop(PF, ahead, more_up, 0)
 
+    speed = jnp.where(k == 0, 12, jnp.where(k == 1, 6, 3))
+
+    def used(i):
+        return jnp.minimum(ND, jnp.where(top, i + 1, ((i + 1) * speed) // 2))
+
     @pl.when(top)
     def _():
         for d in range(NB):
@@ -280,6 +284,12 @@
 
     def stage_part(d):
         handed = d < NB
+
+        @pl.when(top)
+        def _():
+            load_c(d).wait()
+            sib_c(d).wait_recv()
+
         for g in range(2):
             PS[g] = jnp.dot(A[g], group(C, d, g), preferred_element_type=F32)
 
@@ -344,6 +354,11 @@
                         up_fwd(d, m).start()
 
     def stage_dmix(d):
+        @pl.when(below_top)
+        def _():
+            load_c(d).wait()
+            sib_c(d).wait_recv()
+
         load_g(d).wait()
         sib_g(d).wait_recv()
         for g in range(2):
@@ -448,29 +463,21 @@
         for g in range(2):
             ACC3[g] = jnp.zeros((256, 256), F32)
 
-    lead_part = jnp.where(top, 0, LAG)
-    lead_dmix = jnp.where(top, LAG, 0)
-    tail = ND + lead_dmix
+    lead_part = jnp.where(top, 0, 1)
+    tail = jnp.where(top, 2 * ND, (2 * ND + 2) // 3)
 
     def body(i, carry):
-        @pl.when(i + PF < ND)
-        def _():
-            d = i + PF
+        def loads(d, carry):
             load_c(d).start()
             load_g(d).start()
             sib_c(d).start()
             sib_g(d).start()
-
-        @pl.when(i + ahead < ND)
-        def _():
-            start_up(i + ahead)
-
-        @pl.when(i < ND)
-        def _():
-            load_c(i).wait()
-            sib_c(i).wait_recv()
-
-        @pl.when(jnp.logical_and(k == 2, i == NB + LAG))
+            return carry
+
+        lax.fori_loop(jnp.minimum(ND, used(i - 1) + PF), jnp.minimum(ND, used(i) + PF), loads, 0)
+        lax.fori_loop(jnp.minimum(ND, used(i - 1) + ahead), jnp.minimum(ND, used(i) + ahead), more_up, 0)
+
+        @pl.when(jnp.logical_and(k == 2, i == NB + 1))
         def _():
             extract(ACC3, 5, 0, D3X)
             for cc in range(2):
@@ -485,16 +492,17 @@
         def _():
             stage_part(d)
 
-        e = i - lead_dmix
-
-        @pl.when(jnp.logical_and(e >= 0, e < ND))
-        def _():
-            stage_gather(e)
-            stage_dmix(e)
-
-        return carry
-
-    lax.fori_loop(0, ND + LAG + 3, body, 0)
+        def dots(d, carry):
+            stage_gather(d)
+            stage_dmix(d)
+            return carry
+
+        lo = jnp.where(top, jnp.clip(i - ND, 0, ND), used(i - 1))
+        hi = jnp.where(top, jnp.clip(i - ND + 1, 0, ND), used(i))
+        lax.fori_loop(lo, hi, dots, 0)
+        return carry
+
+    lax.fori_loop(0, 2 * ND + 3, body, 0)
 
     def finish(d, carry):
         sib_s(d).wait_recv()

time: 183 us -> 147 us (0.80)
  Pallas kernels: 178 us -> 142 us
    pallas_call x1, Pallas kernels: 178 us -> 142 us  [shards(): pl.pallas_call(functools.partial(kernel, nq), out_shape=(jax.ShapeDtypeSt...]
where the time goes in v2:
time: 147 us
  Pallas kernels  142 us (97%)
  local copies, waits for them, and re-layouts  4.87 us (3%)
    pallas_call x1, Pallas kernels, shards(): pl.pallas_call(functools.partial(kernel, nq), out_shape=(jax.ShapeDtypeSt...  142 us
    unnamed x10, local copies, waits for them, and re-layouts  4.87 us

profile of v2, /device:TPU:1, one launch (start us, length us, event | category | flops | bytes accessed | tf_op | source)
XLA Modules:
  0.0 147.2 jit_solution(10024925528814207531)
XLA Ops:
  0.6 141.7 %dense_back.1 = (bf16[128,6144]{1,0:T(8,128)(2,1)}, f32[32,6144]{1,0:T(8,128)}, f32[32,32]{1,0:T(8,128)}, f32[1,6144]{1,0:T(1,128)}) custom-call(bf16[128,6144]{1,0:T(8,128)(2,1)} %bitcast.13, bf16[4,128,6144]{2,1,0:T(8,128)(2,1)} %bitcast.11, f32[1,6144]{1,0:T(1,128)} %gain_ref.1, bf16[32,6144]{1,0:T(8,128)(2,1)} %bitcast.15, bf16[32,32]{1,0:T(8,128)(2,1)} %bitcast.17), custom_call_target="tpu_custom_call" | custom-call | tf_op jit(solution)/shard_map/dense_back/pallas_call | solution.py:636
  142.3 0.0 copy-start
  142.3 2.8 %copy.13 = bf16[1,128,6144]{2,1,0:T(8,128)(2,1)} copy(bf16[1,128,6144]{2,1,0:T(8,128)(2,1)} %bitcast.12) | data formatting | bytes 3145728
  145.1 0.0 copy-done
  145.1 0.0 copy-start.2
  145.1 0.0 copy-start.1
  145.1 0.9 copy.14
  146.0 0.0 copy-done.2
  146.0 0.6 copy.15
  146.6 0.0 copy-done.1
  146.6 0.6 copy.16
Async XLA Ops:
  142.3 2.8 %copy-start = (f32[32,6144]{1,0:T(8,128)S(1)}, f32[32,6144]{1,0:T(8,128)}, u32[]{:S(2)}) copy-start(f32[32,6144]{1,0:T(8,128)} %get-tuple-element.9) | copy-start | bytes 2359300
  145.1 0.9 copy-start.2
  145.1 1.5 %copy-start.1 = (f32[1,6144]{1,0:T(1,128)S(1)}, f32[1,6144]{1,0:T(1,128)}, u32[]{:S(2)}) copy-start(f32[1,6144]{1,0:T(1,128)} %get-tuple-element.19) | copy-start | bytes 73732

commit v3 on v2

--- a/solution.py
+++ b/solution.py
@@ -44,10 +44,10 @@
     out_ref, gwin_ref, gwout_ref, ggain_ref,
     X, HN, OUT, GG, G, C, CB, PB, R, SR, PS, A, A3, ACC, ACC3,
     PRE, RI, MS, WF, WS, W3, DMT, DM, DMB, D3X, DP, WO,
-    PK, RB, ZF, ZS, ZR, AG,
+    HT, MSG, MR, ZS, ZR, AG,
     x_sem, out_sem, lg_sem, lc_sem, sg_s, sg_r, sc_s, sc_r, up_s, up_r, fw_s, fw_r,
     dn_s, dn_r, cb_s, cb_r, ss_s, ss_r, w_s, w_r, w3_s, w3_r, dm_s, dm_r, d3_s, d3_r,
-    rs_s, rs_r, z_s, z_r, ag_s, ag_r,
+    ht_s, ht_r, ms_s, ms_r, z_s, z_r, ag_s, ag_r,
 ):
     D = x_ref.shape[1]
     DC = D // ND
@@ -138,8 +138,11 @@
     def peer(p):
         return {"dp": 2 * p + zh}
 
-    def rs(p, source):
-        return send(PK.at[p], RB.at[q], rs_s.at[p], rs_r.at[source], peer(p))
+    def turn(p, source):
+        return send(HN.at[:, wide(p)], HT.at[q], ht_s.at[p], ht_r.at[source], peer(p))
+
+    def tell(p, source):
+        return send(MSG, MR.at[q], ms_s.at[p], ms_r.at[source], peer(p))
 
     def swap():
         return send(ZS, ZR, z_s, z_r, {"dp": dp + 1 - 2 * zh})
@@ -214,7 +217,7 @@
 
     lax.fori_loop(PF, ahead, more_up, 0)
 
-    speed = jnp.where(k == 0, 12, jnp.where(k == 1, 6, 3))
+    speed = jnp.where(k < 2, 4, 3)
 
     def used(i):
         return jnp.minimum(ND, jnp.where(top, i + 1, ((i + 1) * speed) // 2))
@@ -242,10 +245,9 @@
         return carry
 
     lax.fori_loop(0, 8, norm_rows, 0)
-    pre = nt(HN[...], win_ref[...])
+    pre = nt(win_ref[...], HN[...])
     PRE[...] = pre
-    hid = gelu(pre).astype(BF16)
-    mixw = jnp.dot(hid, wout_ref[...], preferred_element_type=F32)
+    mixw = tn(gelu(pre).astype(BF16), wout_ref[...])
     mixw = jnp.where((iota((128, 32), 1) & 7) <= s, mixw, 0.0)
     WF[...] = jnp.zeros((128, 128), BF16)
     WF[:, 0:32] = mixw.astype(BF16)
@@ -278,6 +280,13 @@
             A[g] = jnp.where(same, total, 0.0).astype(BF16)
 
     spread(WS, A)
+    HT[q] = HN[:, wide(q)]
+
+    def start_turn(o, carry):
+        turn(around(o), q).start()
+        return carry
+
+    lax.fori_loop(1, nq, start_turn, 0)
 
     def group(ref, d, g):
         return ref[d, :, 32 * g : 32 * g + 32, :].reshape(256, DC)
@@ -395,65 +404,84 @@
 
         dflat = DM[...].reshape(128, 128)[:, 0:32].astype(BF16)
         pre = PRE[...]
-        dpre = (gelu_slope(pre) * nt(dflat, wout_ref[...])).astype(BF16)
+        dpre = (gelu_slope(pre) * nt(wout_ref[...], dflat)).astype(BF16)
         DP[...] = dpre
-        WO[...] = jnp.zeros((32, CW), F32)
-        WO[:, 0:32] = tn(gelu(pre).astype(BF16), dflat)
-        MS[...] = jnp.zeros((128, 1), F32)
-
-        def pack(o, carry):
-            p = around(o)
-            at = wide(p)
-            dh = jnp.dot(DP[...], win_ref[:, at], preferred_element_type=F32)
-            t = dh * (X[:, at].astype(F32) * RI[...])
-            MS[...] = MS[...] + jnp.sum(t * gain_ref[:, at], axis=1, keepdims=True)
-            PK[p, 0:32, :] = tn(DP[...], HN[:, at]).astype(BF16)
-            rid = iota((16, CW), 0)
-            per = 32 // nq
-            tile = jnp.where(rid == 0, jnp.sum(t, axis=0, keepdims=True), 0.0)
-            for e in range(per):
-                tile = jnp.where(rid == 1 + e, WO[pl.ds(per * p + e, 1), :], tile)
-            PK[p, 32:48, :] = tile.astype(BF16)
-
-            @pl.when(o < nq)
-            def _():
-                rs(p, q).start()
-
+        wgrad = jnp.dot(gelu(pre).astype(BF16), dflat, preferred_element_type=F32)
+        MSG[0:32, :] = dpre
+        MSG[32:48, :] = jnp.zeros((16, 128), BF16)
+        MSG[32:48, 0:32] = wgrad[0:16].astype(BF16)
+        MSG[32:48, 32:64] = wgrad[16:32].astype(BF16)
+        MR[q] = MSG[...]
+
+        def give(o, carry):
+            tell(around(o), q).start()
             return carry
 
-        lax.fori_loop(1, nq + 1, pack, 0)
-
+        lax.fori_loop(1, nq, give, 0)
+        along = lax.dot_general(
+            pre * dpre.astype(F32), jnp.ones((32, 128), F32), (((0,), (0,)), ((), ())),
+            precision=lax.Precision.HIGHEST, preferred_element_type=F32,
+        )
+        MS[...] = along[:, 0:1] * (1.0 / D)
+        gates(0, part)
+
+    part = nq // 3
+
+    def gates(lo, hi):
         def gate(p, carry):
             at = wide(p)
-            dn = jnp.dot(DP[...], win_ref[:, at], preferred_element_type=F32) * gain_ref[:, at]
+            dn = tn(DP[...], win_ref[:, at]) * gain_ref[:, at]
             normed = X[:, at].astype(F32) * RI[...]
-            GG[:, at] = RI[...] * (dn - normed * (MS[...] * (1.0 / D)))
+            GG[:, at] = RI[...] * (dn - normed * MS[...])
             return carry
 
-        lax.fori_loop(0, nq, gate, 0)
+        lax.fori_loop(lo, hi, gate, 0)
 
     def stage_sum():
-        ZF[...] = PK[q].astype(F32)
-
-        def add(o, carry):
+        def hear(o, carry):
             p = around(o)
-            rs(0, p).wait_recv()
-            ZF[...] = ZF[...] + RB[p].astype(F32)
+            turn(0, p).wait_recv()
+            tell(0, p).wait_recv()
             return carry
 
-        lax.fori_loop(1, nq, add, 0)
-        ZS[...] = ZF[...].astype(BF16)
+        lax.fori_loop(1, nq, hear, 0)
+        told = jnp.concatenate([MR[p, 0:32, :] for p in range(nq)], axis=1)
+        ZS[0:32, :] = jnp.dot(told, HT[...].reshape(nq * 128, CW), preferred_element_type=F32).astype(BF16)
+        wgrad = sum(MR[p, 32:48, :].astype(F32) for p in range(nq))
+        ZS[32:48, :] = jnp.zeros((16, CW), BF16)
+        ZS[32:48, 0:128] = wgrad.astype(BF16)
         swap().start()
+        gates(part, 2 * part)
 
     def stage_share():
         swap().wait_recv()
-        AG[q] = (ZS[...].astype(F32) + ZR[...].astype(F32)).astype(BF16)
+        both = ZS[...].astype(F32) + ZR[...].astype(F32)
+        AG[q] = both[0:32].astype(BF16)
 
         def give(o, carry):
             ag(around(o), q).start()
             return carry
 
         lax.fori_loop(1, nq, give, 0)
+        WO[...] = both[32:48, 0:128]
+        gates(2 * part, nq)
+
+    def finish(d, carry):
+        sib_s(d).wait_recv()
+        at = cols(d)
+        OUT[half(c), at] = (PB[d, s].astype(F32) + GG[half(c), at]).astype(BF16)
+        OUT[half(1 - c), at] = (SR[d].astype(F32) + GG[half(1 - c), at]).astype(BF16)
+        return carry
+
+    early = 3 * ND // 4
+
+    def store(e):
+        at = slice(0, early * DC) if e == 0 else slice(early * DC, D)
+        return pltpu.make_async_copy(OUT.at[:, at], out_ref.at[:, at], out_sem.at[e])
+
+    def stage_finish():
+        lax.fori_loop(0, early, finish, 0)
+        store(0).start()
 
     @pl.when(k == 2)
     def _():
@@ -486,6 +514,7 @@
         pl.when(i == tail)(stage_grads)
         pl.when(i == tail + 1)(stage_sum)
         pl.when(i == tail + 2)(stage_share)
+        pl.when(i == tail + 3)(stage_finish)
         d = i - lead_part
 
         @pl.when(jnp.logical_and(d >= 0, d < ND))
@@ -502,18 +531,10 @@
         lax.fori_loop(lo, hi, dots, 0)
         return carry
 
-    lax.fori_loop(0, 2 * ND + 3, body, 0)
-
-    def finish(d, carry):
-        sib_s(d).wait_recv()
-        at = cols(d)
-        OUT[half(c), at] = (PB[d, s].astype(F32) + GG[half(c), at]).astype(BF16)
-        OUT[half(1 - c), at] = (SR[d].astype(F32) + GG[half(1 - c), at]).astype(BF16)
-        return carry
-
-    lax.fori_loop(0, ND, finish, 0)
-    store = pltpu.make_async_copy(OUT, out_ref, out_sem)
-    store.start()
+    lax.fori_loop(0, 2 * ND + 4, body, 0)
+
+    lax.fori_loop(early, ND, finish, 0)
+    store(1).start()
 
     def unpack(o, carry):
         p = around(o)
@@ -523,15 +544,14 @@
             ag(0, p).wait_recv()
 
         at = wide(p)
-        gwin_ref[:, at] = AG[p, 0:32, :].astype(F32)
-        extra = AG[p, 32:48, :].astype(F32)
-        ggain_ref[:, at] = extra[0:1]
-        per = 32 // nq
-        for e in range(per):
-            gwout_ref[pl.ds(per * p + e, 1), :] = extra[1 + e : 2 + e, 0:32]
+        m = AG[p].astype(F32)
+        gwin_ref[:, at] = m
+        ggain_ref[:, at] = jnp.sum(m * win_ref[:, at].astype(F32), axis=0, keepdims=True) / gain_ref[:, at]
         return carry
 
     lax.fori_loop(1, nq + 1, unpack, 0)
+    gwout_ref[0:16, :] = WO[:, 0:32]
+    gwout_ref[16:32, :] = WO[:, 32:64]
 
     def drain(d, carry):
         sib_c(d).wait_send()
@@ -574,13 +594,45 @@
 
     def drain_peer(o, carry):
         p = around(o)
-        rs(p, q).wait_send()
+        turn(p, q).wait_send()
+        tell(p, q).wait_send()
         ag(p, q).wait_send()
         return carry
 
     lax.fori_loop(1, nq, drain_peer, 0)
     swap().wait_send()
-    store.wait()
+    for e in range(2):
+        store(e).wait()
+
+
+def copies(g_ref, w_ref, o_ref, n_ref, g_out, w_out, o_out, n_out, G, W, O, N, read, write):
+    rows = G.shape[0] // 4
+    pairs = [(g_ref.at[pl.ds(e * rows, rows)], G.at[pl.ds(e * rows, rows)], g_out.at[pl.ds(e * rows, rows)]) for e in range(4)]
+    rows_w = W.shape[0] // 2
+    pairs += [(w_ref.at[pl.ds(e * rows_w, rows_w)], W.at[pl.ds(e * rows_w, rows_w)], w_out.at[pl.ds(e * rows_w, rows_w)]) for e in range(2)]
+    pairs += [(o_ref, O, o_out), (n_ref, N, n_out)]
+    reads = [pltpu.make_async_copy(a, b, read.at[i]) for i, (a, b, _) in enumerate(pairs)]
+    writes = [pltpu.make_async_copy(b, c, write.at[i]) for i, (_, b, c) in enumerate(pairs)]
+    for move in reads:
+        move.start()
+    for i in range(len(pairs)):
+        reads[i].wait()
+        writes[i].start()
+    for move in writes:
+        move.wait()
+
+
+def hand_over(*arrays):
+    any_space = pl.BlockSpec(memory_space=pl.ANY)
+    return pl.pallas_call(
+        copies,
+        out_shape=tuple(jax.ShapeDtypeStruct(a.shape, a.dtype) for a in arrays),
+        in_specs=[any_space] * len(arrays),
+        out_specs=(any_space,) * len(arrays),
+        scratch_shapes=[pltpu.VMEM(a.shape, a.dtype) for a in arrays] + [pltpu.SemaphoreType.DMA((8,))] * 2,
+        name="hand_over",
+        compiler_params=pltpu.CompilerParams(vmem_limit_bytes=56 << 20),
+    )(*arrays)
 
 
 def shards(outputs, cotangents, gain, w_in, w_out):
@@ -607,7 +659,7 @@
         pltpu.VMEM((2, 256, 256), BF16),
         pltpu.VMEM((2, 256, 256), F32),
         pltpu.VMEM((2, 256, 256), F32),
-        pltpu.VMEM((128, 32), F32),
+        pltpu.VMEM((32, 128), F32),
         pltpu.VMEM((128, 1), F32),
         pltpu.VMEM((128, 1), F32),
         pltpu.VMEM((128, 128), BF16),
@@ -617,21 +669,22 @@
         pltpu.VMEM((2, 64, 128), F32),
         pltpu.VMEM((2, 64, 128), F32),
         pltpu.VMEM((2, 64, 128), F32),
-        pltpu.VMEM((128, 32), BF16),
-        pltpu.VMEM((32, CW), F32),
-        pltpu.VMEM((nq, 48, CW), BF16),
-        pltpu.VMEM((nq, 48, CW), BF16),
-        pltpu.VMEM((48, CW), F32),
+        pltpu.VMEM((32, 128), BF16),
+        pltpu.VMEM((16, 128), F32),
+        pltpu.VMEM((nq, 128, CW), BF16),
+        pltpu.VMEM((48, 128), BF16),
+        pltpu.VMEM((nq, 48, 128), BF16),
         pltpu.VMEM((48, CW), BF16),
         pltpu.VMEM((48, CW), BF16),
-        pltpu.VMEM((nq, 48, CW), BF16),
-        dma, dma, dma((ND,)), dma((ND,)),
+        pltpu.VMEM((nq, 32, CW), BF16),
+        dma, dma((2,)), dma((ND,)), dma((ND,)),
         dma((ND,)), dma((ND,)), dma((ND,)), dma((ND,)),
         dma((ND, 2)), dma((ND, 2)), dma((ND, 2)), dma((ND, 2)),
         dma((ND, 3)), dma((ND, 3)), dma((NB, 2)), dma((NB, 2)),
         dma((ND,)), dma((ND,)), dma, dma, dma((2,)), dma((2,)),
         dma, dma, dma((2,)), dma((2,)),
-        dma((nq,)), dma((nq,)), dma, dma, dma((nq,)), dma((nq,)),
+        dma((nq,)), dma((nq,)), dma((nq,)), dma((nq,)),
+        dma, dma, dma((nq,)), dma((nq,)),
     ]
     grad, gwin, gwout, ggain = pl.pallas_call(
         functools.partial(kernel, nq),
@@ -649,6 +702,7 @@
             collective_id=0, has_side_effects=True, vmem_limit_bytes=56 << 20
         ),
     )(outputs[0], cotangents[0], gain, w_in[0].T, w_out[0])
+    grad, gwin, gwout, ggain = hand_over(grad, gwin, gwout, ggain)
     return grad[None], gwin.T[None], gwout[None], ggain
 
 

time: 147 us -> 144 us (0.980)
  local copies, waits for them, and re-layouts: 4.87 us -> 0 us
    unnamed x10 -> x0, local copies, waits for them, and re-layouts: 4.87 us -> none
    pallas_call x0 -> x1, Pallas kernels: none -> 2.53 us  [hand_over(): pl.pallas_call(copies, out_shape=tuple((jax.ShapeDtypeStruct(a.shape, a.d...]
where the time goes in v3:
time: 144 us
  Pallas kernels  143 us (99%)
    pallas_call x1, Pallas kernels, shards(): pl.pallas_call(functools.partial(kernel, nq), out_shape=(jax.ShapeDtypeSt...  140 us

profile of v3, /device:TPU:1, one launch (start us, length us, event | category | flops | bytes accessed | tf_op | source)
XLA Modules:
  0.0 143.6 jit_solution(3823060011728951249)
XLA Ops:
  0.6 140.4 %dense_back.1 = (bf16[128,6144]{1,0:T(8,128)(2,1)}, f32[32,6144]{1,0:T(8,128)}, f32[32,32]{1,0:T(8,128)}, f32[1,6144]{1,0:T(1,128)}) custom-call(bf16[128,6144]{1,0:T(8,128)(2,1)} %bitcast.12, bf16[4,128,6144]{2,1,0:T(8,128)(2,1)} %bitcast.11, f32[1,6144]{1,0:T(1,128)} %gain_ref.1, bf16[32,6144]{1,0:T(8,128)(2,1)} %bitcast.13, bf16[32,32]{1,0:T(8,128)(2,1)} %bitcast.14), custom_call_target="tpu_custom_call" | custom-call | tf_op jit(solution)/shard_map/dense_back/pallas_call | solution.py:689
  141.1 2.5 %hand_over.1 = (bf16[128,6144]{1,0:T(8,128)(2,1)}, f32[32,6144]{1,0:T(8,128)}, f32[32,32]{1,0:T(8,128)}, f32[1,6144]{1,0:T(1,128)}) custom-call(bf16[128,6144]{1,0:T(8,128)(2,1)} %get-tuple-element.12.g_ref, f32[32,6144]{1,0:T(8,128)} %get-tuple-element.13.w_ref, f32[32,32]{1,0:T(8,128)} %get-tuple-element.14.o_ref, f32[1,6144]{1,0:T(1,128)} %get-tuple-element.15.n_ref), custom_call_target="tpu_custom_call" | custom-call | tf_op jit(solution)/shard_map/hand_over/pallas_call | solution.py:627

commit v4 on v3

--- a/solution.py
+++ b/solution.py
@@ -7,7 +7,7 @@
 from jax.experimental.pallas import tpu as pltpu
 from jax.sharding import PartitionSpec as P
 
-ND = 12
+ND = 8
 NB = 1
 PF = 3
 PF_TOP = 6

time: 144 us -> 132 us (0.917)
  Pallas kernels: 143 us -> 131 us
    pallas_call x1, Pallas kernels: 140 us -> 128 us  [shards(): pl.pallas_call(functools.partial(kernel, nq), out_shape=(jax.ShapeDtypeSt...]
where the time goes in v4:
time: 132 us; the launch traced here: 131 us
  Pallas kernels  131 us (99%)
    pallas_call x1, Pallas kernels, shards(): pl.pallas_call(functools.partial(kernel, nq), out_shape=(jax.ShapeDtypeSt...  128 us

profile of v4, /device:TPU:1, one launch (start us, length us, event | category | flops | bytes accessed | tf_op | source)
XLA Modules:
  0.0 131.2 jit_solution(9257910364507114204)
XLA Ops:
  0.6 128.0 %dense_back.1 = (bf16[128,6144]{1,0:T(8,128)(2,1)}, f32[32,6144]{1,0:T(8,128)}, f32[32,32]{1,0:T(8,128)}, f32[1,6144]{1,0:T(1,128)}) custom-call(bf16[128,6144]{1,0:T(8,128)(2,1)} %bitcast.12, bf16[4,128,6144]{2,1,0:T(8,128)(2,1)} %bitcast.11, f32[1,6144]{1,0:T(1,128)} %gain_ref.1, bf16[32,6144]{1,0:T(8,128)(2,1)} %bitcast.13, bf16[32,32]{1,0:T(8,128)(2,1)} %bitcast.14), custom_call_target="tpu_custom_call" | custom-call | tf_op jit(solution)/shard_map/dense_back/pallas_call | solution.py:689
  128.6 2.5 %hand_over.1 = (bf16[128,6144]{1,0:T(8,128)(2,1)}, f32[32,6144]{1,0:T(8,128)}, f32[32,32]{1,0:T(8,128)}, f32[1,6144]{1,0:T(1,128)}) custom-call(bf16[128,6144]{1,0:T(8,128)(2,1)} %get-tuple-element.12.g_ref, f32[32,6144]{1,0:T(8,128)} %get-tuple-element.13.w_ref, f32[32,32]{1,0:T(8,128)} %get-tuple-element.14.o_ref, f32[1,6144]{1,0:T(1,128)} %get-tuple-element.15.n_ref), custom_call_target="tpu_custom_call" | custom-call | tf_op jit(solution)/shard_map/hand_over/pallas_call | solution.py:627

commit v5 on v4

--- a/solution.py
+++ b/solution.py
@@ -304,6 +304,14 @@
 
         @pl.when(jnp.logical_and(k == 2, handed))
         def _():
+            @pl.when(d == 0)
+            def _():
+                for a in range(2):
+                    top_w(0, a).wait_recv()
+                spread(W3, A3)
+                for g in range(2):
+                    ACC3[g] = jnp.zeros((256, 256), F32)
+
             for a in range(2):
                 hand(d, 0, a).wait_recv()
             for g in range(2):
@@ -483,14 +491,6 @@
         lax.fori_loop(0, early, finish, 0)
         store(0).start()
 
-    @pl.when(k == 2)
-    def _():
-        for a in range(2):
-            top_w(0, a).wait_recv()
-        spread(W3, A3)
-        for g in range(2):
-            ACC3[g] = jnp.zeros((256, 256), F32)
-
     lead_part = jnp.where(top, 0, 1)
     tail = jnp.where(top, 2 * ND, (2 * ND + 2) // 3)
 
@@ -514,7 +514,7 @@
         pl.when(i == tail)(stage_grads)
         pl.when(i == tail + 1)(stage_sum)
         pl.when(i == tail + 2)(stage_share)
-        pl.when(i == tail + 3)(stage_finish)
+        pl.when(i == tail + 2)(stage_finish)
         d = i - lead_part
 
         @pl.when(jnp.logical_and(d >= 0, d < ND))
@@ -531,7 +531,7 @@
         lax.fori_loop(lo, hi, dots, 0)
         return carry
 
-    lax.fori_loop(0, 2 * ND + 4, body, 0)
+    lax.fori_loop(0, 2 * ND + 3, body, 0)
 
     lax.fori_loop(early, ND, finish, 0)
     store(1).start()
@@ -606,10 +606,10 @@
 
 
 def copies(g_ref, w_ref, o_ref, n_ref, g_out, w_out, o_out, n_out, G, W, O, N, read, write):
-    rows = G.shape[0] // 4
-    pairs = [(g_ref.at[pl.ds(e * rows, rows)], G.at[pl.ds(e * rows, rows)], g_out.at[pl.ds(e * rows, rows)]) for e in range(4)]
-    rows_w = W.shape[0] // 2
-    pairs += [(w_ref.at[pl.ds(e * rows_w, rows_w)], W.at[pl.ds(e * rows_w, rows_w)], w_out.at[pl.ds(e * rows_w, rows_w)]) for e in range(2)]
+    rows = G.shape[0] // 8
+    pairs = [(g_ref.at[pl.ds(e * rows, rows)], G.at[pl.ds(e * rows, rows)], g_out.at[pl.ds(e * rows, rows)]) for e in range(8)]
+    rows_w = W.shape[0] // 4
+    pairs += [(w_ref.at[pl.ds(e * rows_w, rows_w)], W.at[pl.ds(e * rows_w, rows_w)], w_out.at[pl.ds(e * rows_w, rows_w)]) for e in range(4)]
     pairs += [(o_ref, O, o_out), (n_ref, N, n_out)]
     reads = [pltpu.make_async_copy(a, b, read.at[i]) for i, (a, b, _) in enumerate(pairs)]
     writes = [pltpu.make_async_copy(b, c, write.at[i]) for i, (_, b, c) in enumerate(pairs)]
@@ -629,7 +629,7 @@
         out_shape=tuple(jax.ShapeDtypeStruct(a.shape, a.dtype) for a in arrays),
         in_specs=[any_space] * len(arrays),
         out_specs=(any_space,) * len(arrays),
-        scratch_shapes=[pltpu.VMEM(a.shape, a.dtype) for a in arrays] + [pltpu.SemaphoreType.DMA((8,))] * 2,
+        scratch_shapes=[pltpu.VMEM(a.shape, a.dtype) for a in arrays] + [pltpu.SemaphoreType.DMA((14,))] * 2,
         name="hand_over",
         compiler_params=pltpu.CompilerParams(vmem_limit_bytes=56 << 20),
     )(*arrays)

time: 132 us -> 132 us (level)
  no operation moved by 1% of the time
where the time goes in v5:
time: 132 us; the launch traced here: 131 us
  Pallas kernels  131 us (99%)
    pallas_call x1, Pallas kernels, shards(): pl.pallas_call(functools.partial(kernel, nq), out_shape=(jax.ShapeDtypeSt...  128 us
    pallas_call x1, Pallas kernels, hand_over(): pl.pallas_call(copies, out_shape=tuple((jax.ShapeDtypeStruct(a.shape, a.d...  2.66 us

profile of v5, /device:TPU:1, one launch (start us, length us, event | category | flops | bytes accessed | tf_op | source)
XLA Modules:
  0.0 131.3 jit_solution(9025349737383558170)
XLA Ops:
  0.6 128.0 %dense_back.1 = (bf16[128,6144]{1,0:T(8,128)(2,1)}, f32[32,6144]{1,0:T(8,128)}, f32[32,32]{1,0:T(8,128)}, f32[1,6144]{1,0:T(1,128)}) custom-call(bf16[128,6144]{1,0:T(8,128)(2,1)} %bitcast.12, bf16[4,128,6144]{2,1,0:T(8,128)(2,1)} %bitcast.11, f32[1,6144]{1,0:T(1,128)} %gain_ref.1, bf16[32,6144]{1,0:T(8,128)(2,1)} %bitcast.13, bf16[32,32]{1,0:T(8,128)(2,1)} %bitcast.14), custom_call_target="tpu_custom_call" | custom-call | tf_op jit(solution)/shard_map/dense_back/pallas_call | solution.py:689
  128.6 2.7 %hand_over.1 = (bf16[128,6144]{1,0:T(8,128)(2,1)}, f32[32,6144]{1,0:T(8,128)}, f32[32,32]{1,0:T(8,128)}, f32[1,6144]{1,0:T(1,128)}) custom-call(bf16[128,6144]{1,0:T(8,128)(2,1)} %get-tuple-element.12.g_ref, f32[32,6144]{1,0:T(8,128)} %get-tuple-element.13.w_ref, f32[32,32]{1,0:T(8,128)} %get-tuple-element.14.o_ref, f32[1,6144]{1,0:T(1,128)} %get-tuple-element.15.n_ref), custom_call_target="tpu_custom_call" | custom-call | tf_op jit(solution)/shard_map/hand_over/pallas_call | solution.py:627
